TPU v7x, 32 devices: a whole 2x2x4 slice. The times are simulated.
32 devices in a mesh: grp: 2 (over x), bl: 16 (over z, y, core).
Axes of the slice: x: 2, y: 2, z: 4, core: 2. Of those that a mesh axis runs over, the one named last changes fastest.
Arguments:
- station_gains: float32 [16, 8, 40, 512], P('grp', None, None, 'bl'), parts along dimension 0, may hold values from -3 to 3
- model_visibilities: bfloat16 [16, 8, 8, 40, 2048], P('grp', None, None, None, 'bl'), parts along dimension 0, may hold values from -0.65625 to 0.65625
- observed: float32 [16, 8, 8, 2048], P('grp', None, None, 'bl'), parts along dimension 0, may hold values from -6 to 6
- weights: float32 [16, 8, 2048], P('grp', None, 'bl'), parts along dimension 0, may hold values from 0.005 to 0.05
- kept_visibility_mask: int32 [16, 8, 2048], P('grp', None, 'bl'), parts along dimension 0, may hold values 0 or 1
- first_station: int32 [2048], P('bl'), may hold values from 0 to 511, as said below
- second_station: int32 [2048], P('bl'), may hold values from 0 to 511, as said below
Outputs:
- gradient: float32 [16, 8, 40, 512], P('grp', None, None, 'bl'), parts along dimension 0
There are 2 independent parts, one for each index of `grp`. A program takes and returns all parts, laid end to end along the dimension named above; an argument that names none is the same for every part. Nothing has to cross between parts.
Inputs may be any that keep to these rules, and one draw needn't show every extreme that they name: Baselines come in blocks of 128; in block k, with h = k // 8 and l = k % 8, every first_station lies in [h * 8 * 32, (h + 1) * 8 * 32), every second_station s has (s // 32) % 8 == l, the two stations of a baseline differ, and no pair repeats within a block. `second_station`: see first_station.
All inputs are finite; a program needn't handle non-finite values. No bound on the sum of `kept_visibility_mask` on one device may be relied on, other than what follows from the above.
Results may differ from a plain program's by a relative error of at most 0.0003.
Values sent between devices are 32-bit elements; how exact they have to be, the bound alone decides.
A program may use at most 64 MiB of HBM per device.

v0:
```python
import jax
import jax.numpy as jnp
from jax import lax
from jax.sharding import PartitionSpec as P


def unpack(array, axis):
    parts = [lax.index_in_dim(array, entry_at, axis, keepdims=False) for entry_at in range(8)]
    return (parts[:4], parts[4:])


def pack(jones, axis):
    return jnp.stack(jones[0] + jones[1], axis)


def jones_product(left_jones, right_jones):
    out_real = []
    out_imag = []
    for row_at in range(2):
        for col_at in range(2):
            total_real = 0.0
            total_imag = 0.0
            for middle in range(2):
                left_real = left_jones[0][2 * row_at + middle]
                left_imag = left_jones[1][2 * row_at + middle]
                right_real = right_jones[0][2 * middle + col_at]
                right_imag = right_jones[1][2 * middle + col_at]
                total_real = total_real + left_real * right_real - left_imag * right_imag
                total_imag = total_imag + left_real * right_imag + left_imag * right_real
            out_real.append(total_real)
            out_imag.append(total_imag)
    return (out_real, out_imag)


def hermitian(jones):
    order_list = [0, 2, 1, 3]
    return (
        [jones[0][entry_at] for entry_at in order_list],
        [-jones[1][entry_at] for entry_at in order_list],
    )


def predict_block(lead_gain, trail_gain, model_block):
    left_jones = unpack(lead_gain[:, None], 2)
    right_jones = unpack(trail_gain[:, None], 2)
    sky_jones = unpack(model_block.astype(jnp.float32), 2)
    predicted = jones_product(jones_product(left_jones, sky_jones), hermitian(right_jones))
    summed = (
        [jnp.sum(part, axis=2) for part in predicted[0]],
        [jnp.sum(part, axis=2) for part in predicted[1]],
    )
    return pack(summed, 2)


def gradient_block(lead_gain, trail_gain, model_block, weighted):
    left_jones = unpack(lead_gain[:, None], 2)
    right_jones = unpack(trail_gain[:, None], 2)
    sky_jones = unpack(model_block.astype(jnp.float32), 2)
    residual = unpack(weighted[:, :, :, None], 2)
    toward_lead = jones_product(residual, jones_product(right_jones, hermitian(sky_jones)))
    toward_trail = jones_product(hermitian(residual), jones_product(left_jones, sky_jones))
    lead_sum = (
        [jnp.sum(part, axis=1) for part in toward_lead[0]],
        [jnp.sum(part, axis=1) for part in toward_lead[1]],
    )
    trail_sum = (
        [jnp.sum(part, axis=1) for part in toward_trail[0]],
        [jnp.sum(part, axis=1) for part in toward_trail[1]],
    )
    return (pack(lead_sum, 1), pack(trail_sum, 1))


def station_rows(array):
    lead_shape = array.shape[:3]
    flat = lead_shape[0] * lead_shape[1] * lead_shape[2]
    return jnp.transpose(array, (3, 0, 1, 2)).reshape(array.shape[3], flat)


def station_last(rows, lead_shape):
    return jnp.transpose(rows.reshape((rows.shape[0],) + lead_shape), (1, 2, 3, 0))


def body(
    station_gains,
    model_visibilities,
    observed,
    weights,
    kept_visibility_mask,
    first_station,
    second_station,
):
    width_bl = lax.axis_size("bl")
    per_device = station_gains.shape[3]
    term_shape = station_gains.shape[:3]
    own_rows = station_rows(station_gains)
    gathered = lax.all_gather(own_rows, "bl", axis=0, tiled=True)
    lead_gain = station_last(jnp.take(gathered, first_station, axis=0), term_shape)
    trail_gain = station_last(jnp.take(gathered, second_station, axis=0), term_shape)
    dir_count = station_gains.shape[2]
    dir_block = 8
    count_of_blocks = dir_count // dir_block
    live_weight = weights * kept_visibility_mask.astype(jnp.float32)

    def predict_step(block_at, running):
        block_start = block_at * dir_block
        lead_part = lax.dynamic_slice_in_dim(lead_gain, block_start, dir_block, 2)
        trail_part = lax.dynamic_slice_in_dim(trail_gain, block_start, dir_block, 2)
        model_block = lax.dynamic_slice_in_dim(model_visibilities, block_start, dir_block, 3)
        return running + predict_block(lead_part, trail_part, model_block)

    predicted = lax.fori_loop(
        0, count_of_blocks, predict_step, jnp.zeros(observed.shape, jnp.float32)
    )
    weighted = (observed - predicted) * live_weight[:, :, None, :]

    def gradient_step(block_at, buffers):
        lead_buffer, trail_buffer = buffers
        block_start = block_at * dir_block
        lead_part = lax.dynamic_slice_in_dim(lead_gain, block_start, dir_block, 2)
        trail_part = lax.dynamic_slice_in_dim(trail_gain, block_start, dir_block, 2)
        model_block = lax.dynamic_slice_in_dim(model_visibilities, block_start, dir_block, 3)
        toward_lead, toward_trail = gradient_block(lead_part, trail_part, model_block, weighted)
        lead_buffer = lax.dynamic_update_slice_in_dim(lead_buffer, toward_lead, block_start, 2)
        trail_buffer = lax.dynamic_update_slice_in_dim(trail_buffer, toward_trail, block_start, 2)
        return (lead_buffer, trail_buffer)

    empty_terms = jnp.zeros(lead_gain.shape, jnp.float32)
    toward_lead, toward_trail = lax.fori_loop(
        0, count_of_blocks, gradient_step, (empty_terms, empty_terms)
    )
    lead_rows = station_rows(toward_lead)
    trail_rows = station_rows(toward_trail)
    flat = lead_rows.shape[1]
    full_sum = jnp.zeros((per_device * width_bl, flat), jnp.float32)
    full_sum = full_sum.at[first_station].add(lead_rows)
    full_sum = full_sum.at[second_station].add(trail_rows)
    owned = lax.psum_scatter(full_sum, "bl", scatter_dimension=0, tiled=True)
    return -station_last(owned, term_shape)


def solution(mesh):
    return jax.shard_map(
        body,
        mesh=mesh,
        in_specs=(
            P("grp", None, None, "bl"),
            P("grp", None, None, None, "bl"),
            P("grp", None, None, "bl"),
            P("grp", None, "bl"),
            P("grp", None, "bl"),
            P("bl"),
            P("bl"),
        ),
        out_specs=P("grp", None, None, "bl"),
        check_vma=False,
    )
```

profile of v0, /device:TPU:0, one launch (start us, length us, event | category | flops | bytes accessed | tf_op | source)
XLA Modules:
  0.0 233.8 jit_solution(7684802133642925480)
XLA Ops:
  6.5 1.8 copy.41
  8.4 1.3 reshape.167
  9.9 58.7 %all-gather.2.cloned.1.call-done = f32[512,2560]{1,0:T(8,128)} async-done(((f32[32,2560]{1,0:T(8,128)}), f32[512,2560]{1,0:T(8,128)}) %all-gather.2.cloned.1.call-update) | async-done | bytes 5242896 | tf_op jit(solution)/shard_map/all_gather | solution.py:96
  68.6 4.1 %gather_fusion.1 = f32[128,2560]{1,0:T(8,128)S(1)} fusion(f32[512,2560]{1,0:T(8,128)} %all-gather.2.cloned.1.call-done, s32[1024]{0:T(1024)S(1)} %pad_clamp_fusion), kind=kCustom, calls=%fused_computation.1.clone | custom fusion | bytes 2621952 | tf_op jit(solution)/shard_map/jit(_take)/gather | solution.py:98
  73.3 4.1 %gather_fusion = f32[128,2560]{1,0:T(8,128)S(1)} fusion(f32[512,2560]{1,0:T(8,128)} %all-gather.2.cloned.1.call-done, s32[1024]{0:T(1024)S(1)} %pad_clamp_fusion.1), kind=kCustom, calls=%fused_computation.clone | custom fusion | bytes 2621952 | tf_op jit(solution)/shard_map/jit(_take)/gather | solution.py:97
  77.4 1.2 broadcast_select_fusion.1
  78.6 1.7 copy.42
  80.3 18.9 %while.31 = (s32[]{:T(128)}, f32[8,8,8,128]{3,2,1,0:T(8,128)S(1)}, f32[8,8,40,128]{3,2,1,0:T(8,128)S(1)}, bf16[8,8,8,40,128]{4,3,2,1,0:T(8,128)(2,1)}, f32[8,8,4...) while((s32[]{:T(128)}, f32[8,8,8,128]{3,2,1,0:T(8,128)S(1)}, ...), condition=%wide.region_9.0_spmd.clone, body=%wide.region_0.10_spmd.clone.sunk | while | flops 8486919 | bytes 18088104 | solution.py:111
  80.5 1.5 dynamic-slice_convert_fusion.5
  82.6 1.0 add_reduce_fusion.17
  84.2 1.5 dynamic-slice_convert_fusion.5
  86.4 1.0 add_reduce_fusion.17
  88.0 1.5 dynamic-slice_convert_fusion.5
  90.1 1.0 add_reduce_fusion.17
  91.8 1.5 dynamic-slice_convert_fusion.5
  93.9 1.0 add_reduce_fusion.17
  95.6 1.5 dynamic-slice_convert_fusion.5
  97.7 1.0 add_reduce_fusion.17
  100.3 1.2 broadcast_in_dim.68.clone
  101.5 1.2 broadcast_in_dim.68
  102.7 27.4 %while.30 = (s32[]{:T(128)}, f32[8,8,40,128]{3,2,1,0:T(8,128)}, f32[8,8,40,128]{3,2,1,0:T(8,128)}, f32[8,8,8,128]{3,2,1,0:T(8,128)S(1)}, f32[8,8,40,128]{3,2,1,0...) while((s32[]{:T(128)}, f32[8,8,40,128]{3,2,1,0:T(8,128)}, ...), condition=%wide.region_27.0_spmd, body=%wide.region_10.28_spmd.sunk | while | flops 16908292 | bytes 30933196 | solution.py:128
  103.0 1.5 dynamic-slice_convert_fusion.4
  108.4 1.5 dynamic-slice_convert_fusion.4
  113.9 1.5 dynamic-slice_convert_fusion.4
  119.4 1.5 dynamic-slice_convert_fusion.4
  124.9 1.5 dynamic-slice_convert_fusion.4
  130.1 1.8 copy.47
  131.9 1.5 copy.46
  133.4 5.8 %scatter_custom_fusion = f32[512,2560]{1,0:T(8,128)} fusion(s32[128]{0:T(128)S(1)} %compare_select_fusion.1, f32[128,2560]{1,0:T(8,128)} %copy.46, f32[]{:T(128)} %constant.91.clone.1), kind=kCustom, calls=%fused_computation.131 | custom fusion | flops 327680 | bytes 5243392 | tf_op jit(solution)/shard_map/scatter-add | solution.py:135
  139.2 7.2 %scatter_fusion = f32[512,2560]{1,0:T(8,128)} fusion(f32[512,2560]{1,0:T(8,128)} %scatter_custom_fusion, s32[128]{0:T(128)S(1)} %compare_select_fusion, f32[128,2560]{1,0:T(8,128)S(1)} %copy.47), kind=kCustom, calls=%fused_computation.3 | custom fusion | flops 327680 | bytes 3932672 | tf_op jit(solution)/shard_map/scatter-add | solution.py:136
  146.4 77.1 %reduce-scatter.2.cloned.1.call-done = f32[32,2560]{1,0:T(8,128)} async-done(((f32[512,2560]{1,0:T(8,128)}), f32[32,2560]{1,0:T(8,128)}) %reduce-scatter.2.cloned.1.call-update) | async-done | bytes 327696 | tf_op jit(solution)/shard_map/reduce_scatter | solution.py:137
  225.3 1.6 copy.48
  (223 shorter events, 28.6 us)
Async XLA Ops:
  6.5 62.0 %all-gather.2.cloned.1.call-start = ((), (), s32[]{:S(2)}) async-start(), calls=%async_computation.1 | async-start | bytes 5570560 | tf_op jit(solution)/shard_map/all_gather | solution.py:96
  8.4 1.4 copy-start.4
  8.4 1.4 copy-start.3
  8.4 1.5 copy-start.1
  8.4 1.5 copy-start.2
  9.7 213.8 %reduce-scatter.2.cloned.1.call-start = ((), (), s32[]{:S(2)}) async-start(), calls=%async_computation.2 | async-start | bytes 5570560 | tf_op jit(solution)/shard_map/reduce_scatter | solution.py:137
  130.1 1.8 copy-start
Sparse Core Ops, SparseCore 0:
  9.8 58.6 all-gather.1
  146.5 76.9 reduce-scatter.1
where the time goes:
time: 235 us; the launch traced here: 234 us
  waiting for transfers between devices  136 us (58%)
  other arithmetic  52.7 us (22%)
  local copies, waits for them, and re-layouts  30.1 us (13%)
  between operations  13.6 us (6%)
    reduce_scatter x1, waiting for transfers between devices, body(): owned = lax.psum_scatter(full_sum, 'bl', scatter_dimension=0, tiled=True)  77.1 us
    all_gather x1, waiting for transfers between devices, body(): gathered = lax.all_gather(own_rows, 'bl', axis=0, tiled=True)  58.7 us
    convert_element_type x5, other arithmetic, predict_block(): sky_jones = unpack(model_block.astype(jnp.float32), 2)  7.38 us
    convert_element_type x5, other arithmetic, gradient_block(): sky_jones = unpack(model_block.astype(jnp.float32), 2)  7.38 us
    scatter-add x1, other arithmetic, body(): full_sum = full_sum.at[second_station].add(trail_rows)  7.16 us
    reduce_sum x10, other arithmetic, gradient_block(): jnp.sum(part, axis=1)  6.14 us
    scatter-add x1, other arithmetic, body(): full_sum = full_sum.at[first_station].add(lead_rows)  5.8 us
    sub x25, other arithmetic, jones_product(): total_real = total_real + left_real * right_real - left_imag * right_imag  5.25 us
  transfers between devices with their start and end apart: 2, of which 2 were waited for; matrix products, arithmetic and copies ran while one was open for 0% of the time, Pallas kernels for 0%

commit v1 on v0

v1 whole, which is shorter than its diff:
```python
import functools

import jax
import jax.numpy as jnp
from jax import lax
from jax.experimental import pallas as pl
from jax.experimental.pallas import tpu as pltpu
from jax.sharding import PartitionSpec as P

GROUP = 8
CHIPS = GROUP // 2
PAIR = 2
F32 = jnp.float32
BF16 = jnp.bfloat16


def split_dot(lhs, rhs, dims, split_left):
    wide = lhs if split_left else rhs
    high = wide.astype(BF16)
    low = (wide - high.astype(F32)).astype(BF16)
    total = None
    for half in (high, low):
        pair = (half, rhs) if split_left else (lhs, half)
        term = lax.dot_general(*pair, (dims, ((), ())), preferred_element_type=F32)
        total = term if total is None else total + term
    return total


def kernel(
    columns,
    per,
    own_ref,
    model_hbm,
    observed_ref,
    weights_ref,
    mask_ref,
    first_ref,
    second_ref,
    out_ref,
    model_ref,
    lead_in,
    trail_in,
    lead_out,
    trail_out,
    pair_in,
    chip_sum,
    chip_in,
    column_in,
    lead_gain,
    trail_gain,
    lead_term,
    trail_term,
    sky,
    outer,
    residual,
    model_sem,
    own_send,
    own_recv,
    relay_send,
    relay_recv,
    back_send,
    back_recv,
):
    steps, padded, flat = own_ref.shape
    channels, times, _, dirs, lanes = model_hbm.shape
    tiles = dirs // 8
    me = lax.axis_index("bl")
    row = me // GROUP
    place = lax.rem(me, GROUP)
    chip = place // 2
    core = lax.rem(place, 2)
    sibling = me + 1 - 2 * core

    def chip_peer(offset):
        return row * GROUP + lax.rem(chip + offset, CHIPS) * 2 + core

    def column_peer(offset):
        return lax.rem(row + offset, columns) * GROUP + place

    peers = [sibling]
    peers += [chip_peer(offset) for offset in range(1, CHIPS)]
    peers += [column_peer(offset) for offset in range(1, columns)]

    def remote(source, target, send, recv, device):
        return pltpu.make_async_remote_copy(
            src_ref=source,
            dst_ref=target,
            send_sem=send,
            recv_sem=recv,
            device_id={"bl": device},
            device_id_type=pl.DeviceIdType.MESH,
        )

    def model_copy(step):
        part = pl.ds(step * PAIR, PAIR)
        return pltpu.make_async_copy(model_hbm.at[part], model_ref.at[part], model_sem.at[step])

    def own_copies(step):
        copies = []
        for at, peer in enumerate(peers):
            if at < CHIPS:
                target = lead_in.at[step, place]
            else:
                target = trail_in.at[step, row]
            copies.append(
                remote(own_ref.at[step], target, own_send.at[step, at], own_recv.at[step, at], peer)
            )
        return copies

    def relay_copies(step):
        copies = []
        for offset in range(1, CHIPS):
            source = lax.rem(chip + CHIPS - offset, CHIPS) * 2 + core
            copies.append(
                remote(
                    lead_in.at[step, source],
                    lead_in.at[step, source],
                    relay_send.at[step, offset - 1],
                    relay_recv.at[step, offset - 1],
                    sibling,
                )
            )
        return copies

    def pair_copies(step):
        return [
            remote(
                lead_out.at[step, at * 2 + 1 - core],
                pair_in.at[step, at],
                back_send.at[step, at],
                back_recv.at[step, at],
                sibling,
            )
            for at in range(CHIPS)
        ]

    def column_copies(step):
        copies = []
        for offset in range(1, columns):
            sem_at = CHIPS + CHIPS - 1 + offset - 1
            copies.append(
                remote(
                    trail_out.at[step, lax.rem(row + offset, columns)],
                    column_in.at[step, offset - 1],
                    back_send.at[step, sem_at],
                    back_recv.at[step, sem_at],
                    column_peer(offset),
                )
            )
        return copies

    def chip_copies(step):
        copies = []
        for offset in range(1, CHIPS):
            sem_at = CHIPS + offset - 1
            copies.append(
                remote(
                    chip_sum.at[step, lax.rem(chip + offset, CHIPS)],
                    chip_in.at[step, offset - 1],
                    back_send.at[step, sem_at],
                    back_recv.at[step, sem_at],
                    chip_peer(offset),
                )
            )
        return copies

    def add_pair(step):
        for copy in pair_copies(step):
            copy.wait_recv()
        for at in range(CHIPS):
            chip_sum[step, at] = lead_out[step, at * 2 + core] + pair_in[step, at]
        for copy in chip_copies(step):
            copy.start()

    def channel(at, step):
        c = step * PAIR + at
        base = at * 8 * dirs

        def rows(q, tile):
            return pl.ds(pl.multiple_of(base + q * dirs + tile * 8, 8), 8)

        def stage(t, carry):
            block = model_ref[c, t].astype(F32)
            sky[t, 0:8] = block
            sky[t, 8:12] = block[0:4] + block[4:8]
            return carry

        lax.fori_loop(0, times, stage, 0)

        def outer_tile(tile, carry):
            lead = [lead_gain[rows(q, tile), :] for q in range(8)]
            trail = [trail_gain[rows(q, tile), :] for q in range(8)]
            for left in range(4):
                for right in range(4):
                    lr, li, tr, ti = lead[left], lead[4 + left], trail[right], trail[4 + right]
                    real = lr * tr + li * ti
                    imag = li * tr - lr * ti
                    slot = (left * 4 + right) * 3
                    outer[tile, slot] = real
                    outer[tile, slot + 1] = imag
                    outer[tile, slot + 2] = real + imag
            return carry

        lax.fori_loop(0, tiles, outer_tile, 0)

        def predict(pair_at, carry):
            sums = [[[None] * 3 for _ in range(4)] for _ in range(2)]
            for tile in range(tiles):
                part = pl.ds(tile * 8, 8)
                for k in range(2):
                    for l in range(2):
                        model = [
                            [sky[pair_at * 2 + u, 4 * z + 2 * k + l, part, :] for z in range(3)]
                            for u in range(2)
                        ]
                        for i in range(2):
                            for j in range(2):
                                slot = ((2 * i + k) * 4 + 2 * j + l) * 3
                                for z in range(3):
                                    gain = outer[tile, slot + z]
                                    for u in range(2):
                                        term = gain * model[u][z]
                                        old = sums[u][2 * i + j][z]
                                        sums[u][2 * i + j][z] = term if old is None else old + term
            for u in range(2):
                t = pair_at * 2 + u
                live = weights_ref[c, pl.ds(t, 1), :] * mask_ref[c, pl.ds(t, 1), :].astype(F32)
                for e in range(4):
                    one, two, three = sums[u][e]
                    real = jnp.sum(one - two, axis=0, keepdims=True)
                    imag = jnp.sum(three - one - two, axis=0, keepdims=True)
                    real = (observed_ref[c, t, e : e + 1, :] - real) * live
                    imag = (observed_ref[c, t, 4 + e : 5 + e, :] - imag) * live
                    residual[t, 3 * e] = jnp.broadcast_to(real, (8, lanes))
                    residual[t, 3 * e + 1] = jnp.broadcast_to(imag, (8, lanes))
                    residual[t, 3 * e + 2] = jnp.broadcast_to(imag - real, (8, lanes))
            return carry

        lax.fori_loop(0, times // 2, predict, 0)

        def gradient(tile, carry):
            part = pl.ds(pl.multiple_of(tile * 8, 8), 8)
            back = [None] * 8

            def add(total, term):
                return term if total is None else total + term

            for i in range(2):
                sums = [[[None] * 3 for _ in range(4)] for _ in range(2)]
                for t in range(times):
                    rest = [
                        [residual[t, 3 * (2 * i + j) + z] for z in range(3)] for j in range(2)
                    ]
                    for e in range(4):
                        for z in range(3):
                            model = sky[t, 4 * z + e, part, :]
                            for j in range(2):
                                sums[j][e][z] = add(sums[j][e][z], rest[j][z] * model)
                front = [None] * 4
                for j in range(2):
                    for e in range(4):
                        k, l = e // 2, e % 2
                        one, two, three = sums[j][e]
                        real = one + two
                        imag = three + (one - two)
                        tr = trail_gain[rows(2 * j + l, tile), :]
                        ti = trail_gain[rows(4 + 2 * j + l, tile), :]
                        lr = lead_gain[rows(2 * i + k, tile), :]
                        li = lead_gain[rows(4 + 2 * i + k, tile), :]
                        front[k] = add(front[k], real * tr - imag * ti)
                        front[2 + k] = add(front[2 + k], real * ti + imag * tr)
                        to = 2 * j + l
                        back[to] = add(back[to], real * lr + imag * li)
                        back[4 + to] = add(back[4 + to], real * li - imag * lr)
                for k in range(2):
                    lead_term[rows(2 * i + k, tile), :] = front[k]
                    lead_term[rows(4 + 2 * i + k, tile), :] = front[2 + k]
            for q in range(8):
                trail_term[rows(q, tile), :] = back[q]
            return carry

        lax.fori_loop(0, tiles, gradient, 0)
        return step

    barrier = pltpu.get_barrier_semaphore()
    for step in range(steps):
        model_copy(step).start()
    for peer in peers:
        pl.semaphore_signal(
            barrier, inc=1, device_id={"bl": peer}, device_id_type=pl.DeviceIdType.MESH
        )
    pl.semaphore_wait(barrier, len(peers))

    def begin(step, carry):
        for copy in own_copies(step):
            copy.start()
        lead_in[step, place] = own_ref[step]
        trail_in[step, row] = own_ref[step]
        return carry

    lax.fori_loop(0, steps, begin, 0)

    def hot(count, ids, leading):
        at = lax.broadcasted_iota(jnp.int32, (count * padded, lanes), 0)
        owner, inner = at // padded, at % padded
        owner = row * GROUP + owner if leading else owner * GROUP + place
        wanted = jnp.where(inner < per, owner * per + inner, -1)
        return jnp.where(wanted == ids, 1.0, 0.0).astype(BF16)

    lead_hot = hot(GROUP, first_ref[...], True)
    trail_hot = hot(columns, second_ref[...], False)
    inner = ((0,), (0,))
    outer_dims = ((1,), (1,))

    def work(step, carry):
        own = own_copies(step)
        relay = relay_copies(step)
        for offset in range(1, CHIPS):
            own[offset].wait_recv()
            relay[offset - 1].start()
        own[0].wait_recv()
        for copy in own[CHIPS:]:
            copy.wait_recv()
        block = trail_in[step].reshape(columns * padded, flat)
        trail_gain[...] = split_dot(block, trail_hot, inner, True)
        model_copy(step).wait()
        for copy in relay:
            copy.wait_recv()
        block = lead_in[step].reshape(GROUP * padded, flat)
        lead_gain[...] = split_dot(block, lead_hot, inner, True)
        lax.fori_loop(0, PAIR, channel, step)
        block = split_dot(lead_hot, lead_term[...], outer_dims, False)
        lead_out[step] = block.reshape(GROUP, padded, flat)
        for copy in pair_copies(step):
            copy.start()
        block = split_dot(trail_hot, trail_term[...], outer_dims, False)
        trail_out[step] = block.reshape(columns, padded, flat)
        for copy in column_copies(step):
            copy.start()
        add_pair(step)
        return carry

    lax.fori_loop(0, steps, work, 0)

    def finish(step, carry):
        total = chip_sum[step, chip] + trail_out[step, row]
        for at, copy in enumerate(column_copies(step)):
            copy.wait_recv()
            total = total + column_in[step, at]
        for at, copy in enumerate(chip_copies(step)):
            copy.wait_recv()
            total = total + chip_in[step, at]
        out_ref[step] = -total
        everything = own_copies(step) + relay_copies(step)
        everything += pair_copies(step) + chip_copies(step) + column_copies(step)
        for copy in everything:
            copy.wait_send()
        return carry

    lax.fori_loop(0, steps, finish, 0)


def body(
    station_gains,
    model_visibilities,
    observed,
    weights,
    kept_visibility_mask,
    first_station,
    second_station,
):
    columns = lax.axis_size("bl") // GROUP
    channels, comps, dirs, per = station_gains.shape
    times, lanes = weights.shape[1], weights.shape[2]
    steps = channels // PAIR
    flat = PAIR * comps * dirs
    padded = max(per, 8)
    own = jnp.transpose(station_gains.reshape(steps, flat, per), (0, 2, 1))
    own = jnp.pad(own, ((0, 0), (0, padded - per), (0, 0)))
    vmem = pl.BlockSpec(memory_space=pltpu.VMEM)
    chunk = (padded, flat)
    backs = CHIPS + CHIPS - 1 + columns - 1
    summed = pl.pallas_call(
        functools.partial(kernel, columns, per),
        out_shape=jax.ShapeDtypeStruct((steps,) + chunk, F32),
        in_specs=[vmem, pl.BlockSpec(memory_space=pl.ANY)] + [vmem] * 5,
        out_specs=vmem,
        scratch_shapes=[
            pltpu.VMEM(model_visibilities.shape, BF16),
            pltpu.VMEM((steps, GROUP) + chunk, F32),
            pltpu.VMEM((steps, columns) + chunk, F32),
            pltpu.VMEM((steps, GROUP) + chunk, F32),
            pltpu.VMEM((steps, columns) + chunk, F32),
            pltpu.VMEM((steps, CHIPS) + chunk, F32),
            pltpu.VMEM((steps, CHIPS) + chunk, F32),
            pltpu.VMEM((steps, CHIPS - 1) + chunk, F32),
            pltpu.VMEM((steps, columns - 1) + chunk, F32),
            pltpu.VMEM((flat, lanes), F32),
            pltpu.VMEM((flat, lanes), F32),
            pltpu.VMEM((flat, lanes), F32),
            pltpu.VMEM((flat, lanes), F32),
            pltpu.VMEM((times, 12, dirs, lanes), F32),
            pltpu.VMEM((dirs // 8, 48, 8, lanes), F32),
            pltpu.VMEM((times, 12, 8, lanes), F32),
            pltpu.SemaphoreType.DMA((steps,)),
            pltpu.SemaphoreType.DMA((steps, CHIPS + columns - 1)),
            pltpu.SemaphoreType.DMA((steps, CHIPS + columns - 1)),
            pltpu.SemaphoreType.DMA((steps, CHIPS - 1)),
            pltpu.SemaphoreType.DMA((steps, CHIPS - 1)),
            pltpu.SemaphoreType.DMA((steps, backs)),
            pltpu.SemaphoreType.DMA((steps, backs)),
        ],
        compiler_params=pltpu.CompilerParams(
            collective_id=0, has_side_effects=True, vmem_limit_bytes=48 * 1024 * 1024
        ),
    )(
        own,
        model_visibilities,
        observed,
        weights,
        kept_visibility_mask,
        first_station.reshape(1, lanes),
        second_station.reshape(1, lanes),
    )
    return jnp.transpose(summed[:, :per], (0, 2, 1)).reshape(station_gains.shape)


def solution(mesh):
    return jax.shard_map(
        body,
        mesh=mesh,
        in_specs=(
            P("grp", None, None, "bl"),
            P("grp", None, None, None, "bl"),
            P("grp", None, None, "bl"),
            P("grp", None, "bl"),
            P("grp", None, "bl"),
            P("bl"),
            P("bl"),
        ),
        out_specs=P("grp", None, None, "bl"),
        check_vma=False,
    )
```

time: 235 us -> 61.4 us (0.26)
  waiting for transfers between devices: 136 us -> 0 us
  other arithmetic: 52.7 us -> 0 us
  Pallas kernels: 0 us -> 51.8 us
  local copies, waits for them, and re-layouts: 30.1 us -> 8.88 us
  between operations: 13.6 us -> 0.04 us
    reduce_scatter x1 -> x0, waiting for transfers between devices: 77.1 us -> none  [body(): owned = lax.psum_scatter(full_sum, 'bl', scatter_dimension=0, tiled=True)]
    all_gather x1 -> x0, waiting for transfers between devices: 58.7 us -> none  [body(): gathered = lax.all_gather(own_rows, 'bl', axis=0, tiled=True)]
    pallas_call x0 -> x1, Pallas kernels: none -> 51.8 us  [body(): pl.pallas_call(functools.partial(kernel, columns, per), out_shape=jax.Sha...]
    convert_element_type x10 -> x0, other arithmetic: 14.8 us -> none  [the longest x5 7.38 us: predict_block(): sky_jones = unpack(model_block.astype(jnp.float32), 2)]
    scatter-add x2 -> x0, other arithmetic: 13 us -> none  [the longest x1 7.16 us: body(): full_sum = full_sum.at[second_station].add(trail_rows)]
    reduce_sum x15 -> x0, other arithmetic: 11.2 us -> none  [the longest x10 6.14 us: gradient_block(): jnp.sum(part, axis=1)]
    gather x2 -> x0, local copies, waits for them, and re-layouts: 8.26 us -> none  [the longest x1 4.14 us: body(): jnp.take(gathered, first_station, axis=0)]
    unnamed x10 -> x11, local copies, waits for them, and re-layouts: 0.03 us -> 5.6 us
  transfers between devices with their start and end apart: 2 -> 0, of which waited for: 2 -> 0; matrix products, arithmetic and copies ran while one was open for 0% -> 0% of each run, Pallas kernels for 0% -> 0%
where the time goes in v1:
time: 61.4 us; the launch traced here: 60.8 us
  Pallas kernels  51.8 us (84%)
  local copies, waits for them, and re-layouts  8.88 us (14%)
    pallas_call x1, Pallas kernels, body(): pl.pallas_call(functools.partial(kernel, columns, per), out_shape=jax.Sha...  51.8 us
    unnamed x11, local copies, waits for them, and re-layouts  5.6 us
    reshape x2, local copies, waits for them, and re-layouts, body(): jnp.transpose(summed[:, :per], (0, 2, 1)).reshape(station_gains.shape)  2.35 us

profile of v1, /device:TPU:0, one launch (start us, length us, event | category | flops | bytes accessed | tf_op | source)
XLA Modules:
  0.0 60.8 jit_solution(16022339905914093527)
XLA Ops:
  0.0 1.8 %copy.8 = f32[8,8,40,32]{2,1,0,3:T(8,128)S(1)} copy(f32[8,8,40,32]{2,3,1,0:T(8,128)} %param.7) | data formatting | bytes 655360 | tf_op args[0]
  1.8 0.7 %reshape.12 = f32[4,640,32]{1,0,2:T(4,128)S(1)} reshape(f32[8,8,40,32]{2,1,0,3:T(8,128)S(1)} %copy.8) | data formatting | bytes 655360 | tf_op jit(solution)/shard_map/reshape | solution.py:378
  2.6 0.0 copy-start
  2.6 0.9 %copy-done = f32[8,8,8,128]{3,2,1,0:T(8,128)S(1)} copy-done((f32[8,8,8,128]{3,2,1,0:T(8,128)S(1)}, f32[8,8,8,128]{3,2,1,0:T(8,128)}, u32[]{:S(2)}) %copy-start) | copy-done | bytes 262168
  3.5 0.0 copy-start.1
  3.5 0.8 %copy-done.1 = f32[8,8,128]{2,1,0:T(8,128)S(1)} copy-done((f32[8,8,128]{2,1,0:T(8,128)S(1)}, f32[8,8,128]{2,1,0:T(8,128)}, u32[]{:S(2)}) %copy-start.1) | copy-done | bytes 32792
  4.3 0.0 copy-start.2
  4.3 0.8 %copy-done.2 = s32[8,8,128]{2,1,0:T(8,128)S(1)} copy-done((s32[8,8,128]{2,1,0:T(8,128)S(1)}, s32[8,8,128]{2,1,0:T(8,128)}, u32[]{:S(2)}) %copy-start.2) | copy-done | bytes 32792
  5.0 0.0 copy-start.3
  5.0 0.7 %copy-done.3 = s32[128]{0:T(128)S(1)} copy-done((s32[128]{0:T(128)S(1)}, s32[128]{0:T(128)}, u32[]{:S(2)}) %copy-start.3) | copy-done | bytes 536
  5.7 0.0 copy-start.4
  5.7 0.7 %copy-done.4 = s32[128]{0:T(128)S(1)} copy-done((s32[128]{0:T(128)S(1)}, s32[128]{0:T(128)}, u32[]{:S(2)}) %copy-start.4) | copy-done | bytes 536
  6.3 51.8 %shard_map.73 = f32[4,32,640]{2,1,0:T(8,128)S(1)} custom-call(f32[4,32,640]{2,1,0:T(8,128)S(1)} %bitcast.12, bf16[8,8,8,40,128]{4,3,2,1,0:T(8,128)(2,1)} %model_hbm.1, f32[8,8,8,128]{3,2,1,0:T(8,128)S(1)} %copy-done, f32[8,8,128]{2,1,0:T(8,128)S(1)} %copy-done.1, s32[8,8,128]{2,1,0:T(8,128)S(1)} %copy-done.2, s32[1,128]{1,0:T(1,128)S(1)} %bitcast.14, ...), custom_call_target="tpu_custom_call" | custom-call | tf_op jit(solution)/shard_map/pallas_call | solution.py:383
  58.2 0.2 copy.10
  58.4 0.8 %reshape.15 = f32[8,8,40,32]{2,1,0,3:T(8,128)S(1)} reshape(f32[4,640,32]{1,0,2:T(4,128)S(1)} %copy.10) | data formatting | bytes 655360 | tf_op jit(solution)/shard_map/reshape | solution.py:425
  59.2 1.6 %copy.11 = f32[8,8,40,32]{2,3,1,0:T(8,128)} copy(f32[8,8,40,32]{2,1,0,3:T(8,128)S(1)} %reshape.15) | data formatting | bytes 655360 | tf_op jit(solution)/shard_map/reshape | solution.py:425
  (1 shorter events, 0.0 us)
Async XLA Ops:
  2.6 1.0 %copy-start = (f32[8,8,8,128]{3,2,1,0:T(8,128)S(1)}, f32[8,8,8,128]{3,2,1,0:T(8,128)}, u32[]{:S(2)}) copy-start(f32[8,8,8,128]{3,2,1,0:T(8,128)} %observed_ref.1) | copy-start | bytes 786436
  3.5 0.8 %copy-start.1 = (f32[8,8,128]{2,1,0:T(8,128)S(1)}, f32[8,8,128]{2,1,0:T(8,128)}, u32[]{:S(2)}) copy-start(f32[8,8,128]{2,1,0:T(8,128)} %weights_ref.1) | copy-start | bytes 98308
  4.3 0.8 %copy-start.2 = (s32[8,8,128]{2,1,0:T(8,128)S(1)}, s32[8,8,128]{2,1,0:T(8,128)}, u32[]{:S(2)}) copy-start(s32[8,8,128]{2,1,0:T(8,128)} %mask_ref.1) | copy-start | bytes 98308
  5.0 0.7 %copy-start.3 = (s32[128]{0:T(128)S(1)}, s32[128]{0:T(128)}, u32[]{:S(2)}) copy-start(s32[128]{0:T(128)} %param.12) | copy-start | bytes 1540
  5.7 0.7 %copy-start.4 = (s32[128]{0:T(128)S(1)}, s32[128]{0:T(128)}, u32[]{:S(2)}) copy-start(s32[128]{0:T(128)} %param.13) | copy-start | bytes 1540

commit v2 on v1

--- a/solution.py
+++ b/solution.py
@@ -29,22 +29,31 @@
 def kernel(
     columns,
     per,
-    own_ref,
+    gains_hbm,
     model_hbm,
+    observed_hbm,
+    weights_hbm,
+    mask_hbm,
+    first_hbm,
+    second_hbm,
+    out_ref,
+    gains_ref,
+    model_ref,
     observed_ref,
     weights_ref,
     mask_ref,
     first_ref,
     second_ref,
-    out_ref,
-    model_ref,
+    own_ref,
     lead_in,
     trail_in,
     lead_out,
     trail_out,
     pair_in,
     chip_sum,
-    chip_in,
+    y_in,
+    z_out,
+    z_in,
     column_in,
     lead_gain,
     trail_gain,
@@ -53,11 +62,11 @@
     sky,
     outer,
     residual,
+    gains_sem,
     model_sem,
-    own_send,
-    own_recv,
-    relay_send,
-    relay_recv,
+    small_sem,
+    go_send,
+    go_recv,
     back_send,
     back_recv,
 ):
@@ -67,18 +76,26 @@
     me = lax.axis_index("bl")
     row = me // GROUP
     place = lax.rem(me, GROUP)
-    chip = place // 2
+    upper = place // 4
+    lower = lax.rem(place // 2, 2)
     core = lax.rem(place, 2)
-    sibling = me + 1 - 2 * core
-
-    def chip_peer(offset):
-        return row * GROUP + lax.rem(chip + offset, CHIPS) * 2 + core
+
+    def at_place(up, low, side):
+        return up * 4 + low * 2 + side
+
+    sib_place = at_place(upper, lower, 1 - core)
+    y_place = at_place(upper, 1 - lower, core)
+    z_place = at_place(1 - upper, lower, core)
+    far_place = at_place(1 - upper, 1 - lower, core)
+    base_device = row * GROUP
+    sibling = base_device + sib_place
+    y_peer = base_device + y_place
+    z_peer = base_device + z_place
 
     def column_peer(offset):
         return lax.rem(row + offset, columns) * GROUP + place
 
-    peers = [sibling]
-    peers += [chip_peer(offset) for offset in range(1, CHIPS)]
+    peers = [sibling, y_peer, z_peer]
     peers += [column_peer(offset) for offset in range(1, columns)]
 
     def remote(source, target, send, recv, device):
@@ -95,82 +112,131 @@
         part = pl.ds(step * PAIR, PAIR)
         return pltpu.make_async_copy(model_hbm.at[part], model_ref.at[part], model_sem.at[step])
 
-    def own_copies(step):
-        copies = []
-        for at, peer in enumerate(peers):
-            if at < CHIPS:
-                target = lead_in.at[step, place]
-            else:
-                target = trail_in.at[step, row]
-            copies.append(
-                remote(own_ref.at[step], target, own_send.at[step, at], own_recv.at[step, at], peer)
+    def gains_copy(step):
+        part = pl.ds(step * PAIR, PAIR)
+        return pltpu.make_async_copy(gains_hbm.at[part], gains_ref.at[part], gains_sem.at[step])
+
+    small = [
+        pltpu.make_async_copy(source, target, small_sem.at[at])
+        for at, (source, target) in enumerate(
+            (
+                (first_hbm, first_ref),
+                (second_hbm, second_ref),
+                (observed_hbm, observed_ref),
+                (weights_hbm, weights_ref),
+                (mask_hbm, mask_ref),
             )
-        return copies
-
-    def relay_copies(step):
-        copies = []
-        for offset in range(1, CHIPS):
-            source = lax.rem(chip + CHIPS - offset, CHIPS) * 2 + core
-            copies.append(
-                remote(
-                    lead_in.at[step, source],
-                    lead_in.at[step, source],
-                    relay_send.at[step, offset - 1],
-                    relay_recv.at[step, offset - 1],
-                    sibling,
-                )
-            )
-        return copies
+        )
+    ]
+
+    def go(step, at, source, target, device):
+        return remote(source, target, go_send.at[step, at], go_recv.at[step, at], device)
+
+    def relay(step, at, slot, device):
+        return go(step, at, lead_in.at[step, slot], lead_in.at[step, slot], device)
+
+    def own_to(step, at, device):
+        return go(step, at, own_ref.at[step], lead_in.at[step, place], device)
+
+    def go_sib(step):
+        return own_to(step, 0, sibling)
+
+    def go_y(step):
+        return own_to(step, 1, y_peer)
+
+    def go_z(step):
+        return own_to(step, 2, z_peer)
+
+    def go_far(step):
+        return relay(step, 3, z_place, y_peer)
+
+    def pass_y(step):
+        return relay(step, 4, y_place, sibling)
+
+    def pass_z(step):
+        return relay(step, 5, z_place, sibling)
+
+    def pass_far(step):
+        return relay(step, 6, far_place, sibling)
+
+    def go_columns(step):
+        return [
+            go(step, 6 + offset, own_ref.at[step], trail_in.at[step, row], column_peer(offset))
+            for offset in range(1, columns)
+        ]
+
+    def send_own(step):
+        go_z(step).start()
+        go_y(step).start()
+        for copy in go_columns(step):
+            copy.start()
+        go_sib(step).start()
+
+    def pass_near(step):
+        go_z(step).wait_recv()
+        go_far(step).start()
+        pass_z(step).start()
+        go_y(step).wait_recv()
+        pass_y(step).start()
+
+    def pass_last(step):
+        go_far(step).wait_recv()
+        pass_far(step).start()
+
+    def back(step, at, source, target, device):
+        return remote(source, target, back_send.at[step, at], back_recv.at[step, at], device)
 
     def pair_copies(step):
         return [
-            remote(
-                lead_out.at[step, at * 2 + 1 - core],
-                pair_in.at[step, at],
-                back_send.at[step, at],
-                back_recv.at[step, at],
-                sibling,
+            back(
+                step, at, lead_out.at[step, at * 2 + 1 - core], pair_in.at[step, at], sibling
             )
             for at in range(CHIPS)
         ]
 
+    def y_copies(step):
+        return [
+            back(step, CHIPS, chip_sum.at[step, far_place // 2], y_in.at[step, 1], y_peer),
+            back(step, CHIPS + 1, chip_sum.at[step, y_place // 2], y_in.at[step, 0], y_peer),
+        ]
+
+    def z_copy(step):
+        return back(step, CHIPS + 2, z_out.at[step], z_in.at[step], z_peer)
+
     def column_copies(step):
-        copies = []
-        for offset in range(1, columns):
-            sem_at = CHIPS + CHIPS - 1 + offset - 1
-            copies.append(
-                remote(
-                    trail_out.at[step, lax.rem(row + offset, columns)],
-                    column_in.at[step, offset - 1],
-                    back_send.at[step, sem_at],
-                    back_recv.at[step, sem_at],
-                    column_peer(offset),
-                )
+        return [
+            back(
+                step,
+                CHIPS + 2 + offset,
+                trail_out.at[step, lax.rem(row + offset, columns)],
+                column_in.at[step, offset - 1],
+                column_peer(offset),
             )
-        return copies
-
-    def chip_copies(step):
-        copies = []
-        for offset in range(1, CHIPS):
-            sem_at = CHIPS + offset - 1
-            copies.append(
-                remote(
-                    chip_sum.at[step, lax.rem(chip + offset, CHIPS)],
-                    chip_in.at[step, offset - 1],
-                    back_send.at[step, sem_at],
-                    back_recv.at[step, sem_at],
-                    chip_peer(offset),
-                )
-            )
-        return copies
+            for offset in range(1, columns)
+        ]
 
     def add_pair(step):
         for copy in pair_copies(step):
             copy.wait_recv()
         for at in range(CHIPS):
             chip_sum[step, at] = lead_out[step, at * 2 + core] + pair_in[step, at]
-        for copy in chip_copies(step):
+        for copy in y_copies(step):
             copy.start()
+
+    def add_y(step):
+        for copy in y_copies(step):
+            copy.wait_recv()
+        z_out[step] = chip_sum[step, z_place // 2] + y_in[step, 1]
+        z_copy(step).start()
+
+    def pack(step):
+        gains_copy(step).wait()
+        own = jnp.concatenate(
+            [gains_ref[step * PAIR + at, q] for at in range(PAIR) for q in range(8)], axis=1
+        )
+        own_ref[step] = own
+        lead_in[step, place] = own
+        trail_in[step, row] = own
 
     def channel(at, step):
         c = step * PAIR + at
@@ -280,25 +346,23 @@
             return carry
 
         lax.fori_loop(0, tiles, gradient, 0)
-        return step
-
-    barrier = pltpu.get_barrier_semaphore()
+
+    for step in range(steps):
+        gains_copy(step).start()
+    for copy in small:
+        copy.start()
     for step in range(steps):
         model_copy(step).start()
+    barrier = pltpu.get_barrier_semaphore()
     for peer in peers:
         pl.semaphore_signal(
             barrier, inc=1, device_id={"bl": peer}, device_id_type=pl.DeviceIdType.MESH
         )
+    pack(0)
     pl.semaphore_wait(barrier, len(peers))
-
-    def begin(step, carry):
-        for copy in own_copies(step):
-            copy.start()
-        lead_in[step, place] = own_ref[step]
-        trail_in[step, row] = own_ref[step]
-        return carry
-
-    lax.fori_loop(0, steps, begin, 0)
+    send_own(0)
+    for step in range(1, steps):
+        pack(step)
 
     def hot(count, ids, leading):
         at = lax.broadcasted_iota(jnp.int32, (count * padded, lanes), 0)
@@ -307,52 +371,80 @@
         wanted = jnp.where(inner < per, owner * per + inner, -1)
         return jnp.where(wanted == ids, 1.0, 0.0).astype(BF16)
 
+    for copy in small:
+        copy.wait()
     lead_hot = hot(GROUP, first_ref[...], True)
     trail_hot = hot(columns, second_ref[...], False)
     inner = ((0,), (0,))
     outer_dims = ((1,), (1,))
+    pass_near(0)
+    if steps > 1:
+        send_own(1)
+    pass_last(0)
 
     def work(step, carry):
-        own = own_copies(step)
-        relay = relay_copies(step)
-        for offset in range(1, CHIPS):
-            own[offset].wait_recv()
-            relay[offset - 1].start()
-        own[0].wait_recv()
-        for copy in own[CHIPS:]:
+        for copy in go_columns(step):
             copy.wait_recv()
         block = trail_in[step].reshape(columns * padded, flat)
         trail_gain[...] = split_dot(block, trail_hot, inner, True)
         model_copy(step).wait()
-        for copy in relay:
+        for copy in (go_sib(step), pass_y(step), pass_z(step), pass_far(step)):
             copy.wait_recv()
         block = lead_in[step].reshape(GROUP * padded, flat)
         lead_gain[...] = split_dot(block, lead_hot, inner, True)
-        lax.fori_loop(0, PAIR, channel, step)
+        channel(0, step)
+
+        @pl.when(step + 1 < steps)
+        def _():
+            pass_near(step + 1)
+
+        @pl.when(step + 2 < steps)
+        def _():
+            send_own(step + 2)
+
+        @pl.when(step >= 1)
+        def _():
+            add_pair(step - 1)
+
+        channel(1, step)
         block = split_dot(lead_hot, lead_term[...], outer_dims, False)
         lead_out[step] = block.reshape(GROUP, padded, flat)
         for copy in pair_copies(step):
             copy.start()
+
+        @pl.when(step + 1 < steps)
+        def _():
+            pass_last(step + 1)
+
         block = split_dot(trail_hot, trail_term[...], outer_dims, False)
         trail_out[step] = block.reshape(columns, padded, flat)
         for copy in column_copies(step):
             copy.start()
-        add_pair(step)
+
+        @pl.when(step >= 1)
+        def _():
+            add_y(step - 1)
+
         return carry
 
     lax.fori_loop(0, steps, work, 0)
+    add_pair(steps - 1)
+    add_y(steps - 1)
 
     def finish(step, carry):
-        total = chip_sum[step, chip] + trail_out[step, row]
+        total = chip_sum[step, place // 2] + trail_out[step, row]
         for at, copy in enumerate(column_copies(step)):
             copy.wait_recv()
             total = total + column_in[step, at]
-        for at, copy in enumerate(chip_copies(step)):
-            copy.wait_recv()
-            total = total + chip_in[step, at]
-        out_ref[step] = -total
-        everything = own_copies(step) + relay_copies(step)
-        everything += pair_copies(step) + chip_copies(step) + column_copies(step)
+        z_copy(step).wait_recv()
+        total = -(total + y_in[step, 0] + z_in[step])
+        for at in range(PAIR):
+            for q in range(8):
+                start = (at * 8 + q) * dirs
+                out_ref[step * PAIR + at, q] = total[:, start : start + dirs]
+        everything = [go_sib(step), go_y(step), go_z(step), go_far(step)]
+        everything += [pass_y(step), pass_z(step), pass_far(step), z_copy(step)]
+        everything += go_columns(step) + pair_copies(step) + y_copies(step) + column_copies(step)
         for copy in everything:
             copy.wait_send()
         return carry
@@ -375,26 +467,40 @@
     steps = channels // PAIR
     flat = PAIR * comps * dirs
     padded = max(per, 8)
-    own = jnp.transpose(station_gains.reshape(steps, flat, per), (0, 2, 1))
-    own = jnp.pad(own, ((0, 0), (0, padded - per), (0, 0)))
-    vmem = pl.BlockSpec(memory_space=pltpu.VMEM)
+    gains = jnp.transpose(station_gains, (0, 1, 3, 2))
+    gains = jnp.pad(gains, ((0, 0), (0, 0), (0, padded - per), (0, 0)))
     chunk = (padded, flat)
-    backs = CHIPS + CHIPS - 1 + columns - 1
+
+    def buffer(*lead):
+        return pltpu.VMEM(lead + chunk, F32)
+
+    def sems(*dims):
+        return pltpu.SemaphoreType.DMA(dims)
+
     summed = pl.pallas_call(
         functools.partial(kernel, columns, per),
-        out_shape=jax.ShapeDtypeStruct((steps,) + chunk, F32),
-        in_specs=[vmem, pl.BlockSpec(memory_space=pl.ANY)] + [vmem] * 5,
-        out_specs=vmem,
+        out_shape=jax.ShapeDtypeStruct(gains.shape, F32),
+        in_specs=[pl.BlockSpec(memory_space=pl.ANY)] * 7,
+        out_specs=pl.BlockSpec(memory_space=pltpu.VMEM),
         scratch_shapes=[
+            pltpu.VMEM(gains.shape, F32),
             pltpu.VMEM(model_visibilities.shape, BF16),
-            pltpu.VMEM((steps, GROUP) + chunk, F32),
-            pltpu.VMEM((steps, columns) + chunk, F32),
-            pltpu.VMEM((steps, GROUP) + chunk, F32),
-            pltpu.VMEM((steps, columns) + chunk, F32),
-            pltpu.VMEM((steps, CHIPS) + chunk, F32),
-            pltpu.VMEM((steps, CHIPS) + chunk, F32),
-            pltpu.VMEM((steps, CHIPS - 1) + chunk, F32),
-            pltpu.VMEM((steps, columns - 1) + chunk, F32),
+            pltpu.VMEM(observed.shape, F32),
+            pltpu.VMEM(weights.shape, F32),
+            pltpu.VMEM(weights.shape, jnp.int32),
+            pltpu.VMEM((1, lanes), jnp.int32),
+            pltpu.VMEM((1, lanes), jnp.int32),
+            buffer(steps),
+            buffer(steps, GROUP),
+            buffer(steps, columns),
+            buffer(steps, GROUP),
+            buffer(steps, columns),
+            buffer(steps, CHIPS),
+            buffer(steps, CHIPS),
+            buffer(steps, 2),
+            buffer(steps),
+            buffer(steps),
+            buffer(steps, columns - 1),
             pltpu.VMEM((flat, lanes), F32),
             pltpu.VMEM((flat, lanes), F32),
             pltpu.VMEM((flat, lanes), F32),
@@ -402,19 +508,19 @@
             pltpu.VMEM((times, 12, dirs, lanes), F32),
             pltpu.VMEM((dirs // 8, 48, 8, lanes), F32),
             pltpu.VMEM((times, 12, 8, lanes), F32),
-            pltpu.SemaphoreType.DMA((steps,)),
-            pltpu.SemaphoreType.DMA((steps, CHIPS + columns - 1)),
-            pltpu.SemaphoreType.DMA((steps, CHIPS + columns - 1)),
-            pltpu.SemaphoreType.DMA((steps, CHIPS - 1)),
-            pltpu.SemaphoreType.DMA((steps, CHIPS - 1)),
-            pltpu.SemaphoreType.DMA((steps, backs)),
-            pltpu.SemaphoreType.DMA((steps, backs)),
+            sems(steps),
+            sems(steps),
+            sems(5),
+            sems(steps, 6 + columns),
+            sems(steps, 6 + columns),
+            sems(steps, CHIPS + 2 + columns),
+            sems(steps, CHIPS + 2 + columns),
         ],
         compiler_params=pltpu.CompilerParams(
-            collective_id=0, has_side_effects=True, vmem_limit_bytes=48 * 1024 * 1024
+            collective_id=0, has_side_effects=True, vmem_limit_bytes=60 * 1024 * 1024
         ),
     )(
-        own,
+        gains,
         model_visibilities,
         observed,
         weights,
@@ -422,7 +528,7 @@
         first_station.reshape(1, lanes),
         second_station.reshape(1, lanes),
     )
-    return jnp.transpose(summed[:, :per], (0, 2, 1)).reshape(station_gains.shape)
+    return jnp.transpose(summed[:, :, :per], (0, 1, 3, 2))
 
 
 def solution(mesh):

time: 61.4 us -> 61.9 us (level)
  Pallas kernels: 51.8 us -> 59.4 us
  local copies, waits for them, and re-layouts: 8.88 us -> 2.26 us
    pallas_call x1, Pallas kernels: 51.8 us -> 59.4 us  [body(): pl.pallas_call(functools.partial(kernel, columns, per), out_shape=jax.Sha...]
    unnamed x11 -> x1, local copies, waits for them, and re-layouts: 5.6 us -> 2.26 us
    reshape x4 -> x0, local copies, waits for them, and re-layouts: 3.06 us -> none  [the longest x2 2.35 us: body(): jnp.transpose(summed[:, :per], (0, 2, 1)).reshape(station_gains.shape)]
where the time goes in v2:
time: 61.9 us; the launch traced here: 61.7 us
  Pallas kernels  59.4 us (96%)
  local copies, waits for them, and re-layouts  2.26 us (4%)
    pallas_call x1, Pallas kernels, body(): pl.pallas_call(functools.partial(kernel, columns, per), out_shape=jax.Sha...  59.4 us
    unnamed x1, local copies, waits for them, and re-layouts  2.26 us

profile of v2, /device:TPU:0, one launch (start us, length us, event | category | flops | bytes accessed | tf_op | source)
XLA Modules:
  0.0 61.7 jit_solution(14329355286550903165)
XLA Ops:
  0.0 59.4 %shard_map.73 = f32[8,8,32,40]{3,2,1,0:T(8,128)} custom-call(f32[8,8,32,40]{3,2,1,0:T(8,128)} %bitcast.5, bf16[8,8,8,40,128]{4,3,2,1,0:T(8,128)(2,1)} %model_hbm.1, f32[8,8,8,128]{3,2,1,0:T(8,128)} %observed_hbm.1, f32[8,8,128]{2,1,0:T(8,128)} %weights_hbm.1, s32[8,8,128]{2,1,0:T(8,128)} %mask_hbm.1, s32[1,128]{1,0:T(1,128)} %bitcast.6, s32[1,128]{1,0:T(1,128)} %bitcast.7), custom_call_target="tpu_custom_call" | custom-call | tf_op jit(solution)/shard_map/pallas_call | solution.py:480
  59.4 2.3 %copy.9 = f32[8,8,40,32]{2,3,1,0:T(8,128)} copy(f32[8,8,40,32]{2,3,1,0:T(8,128)} %bitcast.4) | data formatting | bytes 655360

commit v3 on v2

--- a/solution.py
+++ b/solution.py
@@ -71,6 +71,7 @@
     back_recv,
 ):
     steps, padded, flat = own_ref.shape
+    assert steps == 4
     channels, times, _, dirs, lanes = model_hbm.shape
     tiles = dirs // 8
     me = lax.axis_index("bl")
@@ -95,7 +96,7 @@
     def column_peer(offset):
         return lax.rem(row + offset, columns) * GROUP + place
 
-    peers = [sibling, y_peer, z_peer]
+    peers = [sibling, y_peer, z_peer, base_device + far_place]
     peers += [column_peer(offset) for offset in range(1, columns)]
 
     def remote(source, target, send, recv, device):
@@ -148,7 +149,7 @@
         return own_to(step, 2, z_peer)
 
     def go_far(step):
-        return relay(step, 3, z_place, y_peer)
+        return own_to(step, 3, base_device + far_place)
 
     def pass_y(step):
         return relay(step, 4, y_place, sibling)
@@ -168,13 +169,13 @@
     def send_own(step):
         go_z(step).start()
         go_y(step).start()
+        go_far(step).start()
         for copy in go_columns(step):
             copy.start()
         go_sib(step).start()
 
     def pass_near(step):
         go_z(step).wait_recv()
-        go_far(step).start()
         pass_z(step).start()
         go_y(step).wait_recv()
         pass_y(step).start()
@@ -378,8 +379,7 @@
     inner = ((0,), (0,))
     outer_dims = ((1,), (1,))
     pass_near(0)
-    if steps > 1:
-        send_own(1)
+    send_own(1)
     pass_last(0)
 
     def work(step, carry):
@@ -392,19 +392,21 @@
             copy.wait_recv()
         block = lead_in[step].reshape(GROUP * padded, flat)
         lead_gain[...] = split_dot(block, lead_hot, inner, True)
+
+        @pl.when(step >= 1)
+        def _():
+            add_pair(step - 1)
+
         channel(0, step)
 
-        @pl.when(step + 1 < steps)
-        def _():
-            pass_near(step + 1)
-
-        @pl.when(step + 2 < steps)
-        def _():
-            send_own(step + 2)
-
-        @pl.when(step >= 1)
-        def _():
-            add_pair(step - 1)
+        @pl.when(step == 0)
+        def _():
+            pass_near(1)
+            send_own(2)
+
+        @pl.when(step == 1)
+        def _():
+            pass_near(2)
 
         channel(1, step)
         block = split_dot(lead_hot, lead_term[...], outer_dims, False)
@@ -412,14 +414,22 @@
         for copy in pair_copies(step):
             copy.start()
 
-        @pl.when(step + 1 < steps)
-        def _():
-            pass_last(step + 1)
+        @pl.when(step == 0)
+        def _():
+            send_own(3)
 
         block = split_dot(trail_hot, trail_term[...], outer_dims, False)
         trail_out[step] = block.reshape(columns, padded, flat)
         for copy in column_copies(step):
             copy.start()
+
+        @pl.when(step + 1 < steps)
+        def _():
+            pass_last(step + 1)
+
+        @pl.when(step == 1)
+        def _():
+            pass_near(3)
 
         @pl.when(step >= 1)
         def _():

time: 61.9 us -> 54.7 us (0.88)
  Pallas kernels: 59.4 us -> 52.3 us
    pallas_call x1, Pallas kernels: 59.4 us -> 52.3 us  [body(): pl.pallas_call(functools.partial(kernel, columns, per), out_shape=jax.Sha...]
where the time goes in v3:
time: 54.7 us; the launch traced here: 54.6 us
  Pallas kernels  52.3 us (96%)
  local copies, waits for them, and re-layouts  2.26 us (4%)
    pallas_call x1, Pallas kernels, body(): pl.pallas_call(functools.partial(kernel, columns, per), out_shape=jax.Sha...  52.3 us
    unnamed x1, local copies, waits for them, and re-layouts  2.26 us

profile of v3, /device:TPU:0, one launch (start us, length us, event | category | flops | bytes accessed | tf_op | source)
XLA Modules:
  0.0 54.6 jit_solution(16154157100003094668)
XLA Ops:
  0.0 52.3 %shard_map.73 = f32[8,8,32,40]{3,2,1,0:T(8,128)} custom-call(f32[8,8,32,40]{3,2,1,0:T(8,128)} %bitcast.5, bf16[8,8,8,40,128]{4,3,2,1,0:T(8,128)(2,1)} %model_hbm.1, f32[8,8,8,128]{3,2,1,0:T(8,128)} %observed_hbm.1, f32[8,8,128]{2,1,0:T(8,128)} %weights_hbm.1, s32[8,8,128]{2,1,0:T(8,128)} %mask_hbm.1, s32[1,128]{1,0:T(1,128)} %bitcast.6, s32[1,128]{1,0:T(1,128)} %bitcast.7), custom_call_target="tpu_custom_call" | custom-call | tf_op jit(solution)/shard_map/pallas_call | solution.py:490
  52.3 2.3 %copy.9 = f32[8,8,40,32]{2,3,1,0:T(8,128)} copy(f32[8,8,40,32]{2,3,1,0:T(8,128)} %bitcast.4) | data formatting | bytes 655360
